TPU v7x, 32 devices: a whole 2x2x4 slice. The times are simulated.
32 devices in a mesh: wide: 8 (over y, x, core), narrow: 4 (over z).
Axes of the slice: x: 2, y: 2, z: 4, core: 2. Of those that a mesh axis runs over, the one named last changes fastest.
Arguments:
- weights_in: float32 [16, 32, 64, 2, 8, 128], P('wide', 'narrow'), may hold values from -6 to 6
- medium_speed: float32 [8, 8], replicated, may hold values from 0.5 to 2
- target_order: int32 [64], replicated, may hold values from 0 to 63, each once
Outputs:
- weights_out: float32 [16, 64, 32, 2, 8, 128], P('wide', 'narrow')
Inputs may be any that keep to these rules, and one draw needn't show every extreme that they name: `target_order`: a permutation of the 64 starting target boxes.
All inputs are finite; a program needn't handle non-finite values.
Results may differ from a plain program's by a relative error of at most 0.0003.
Values sent between devices are 32-bit elements; how exact they have to be, the bound alone decides.
A program may use at most 192 MiB of HBM per device.

v0:
```python
import jax
import jax.numpy as jnp
from jax import lax
from jax.sharding import PartitionSpec as P

TX = 8
TY = 8
SYH = 4


level_bits = (3, 2, 1, 0)
merges_across = (1, 1, 2, 2)
merges_down = (0, 1, 1, 2)


def swapped(value, axis, stride):
    mask = 2**stride
    pairs = [(source, source ^ mask) for source in range(lax.axis_size(axis))]
    return lax.ppermute(value, axis, pairs)


def cheb_nodes():
    counter = jnp.arange(8, dtype=jnp.float32)
    return 0.5 - 0.5 * jnp.cos(jnp.pi * (2.0 * counter + 1.0) / 16.0)


def lagrange_matrix(child_bit):
    node_set = cheb_nodes()
    points = (child_bit.astype(jnp.float32) + node_set) / 2.0
    differ = points[None, :, None] - node_set[None, None, :]
    spacing = node_set[:, None] - node_set[None, :]
    diagonal = jnp.eye(8, dtype=bool)
    factors = jnp.where(
        diagonal[:, None, :], 1.0, differ / jnp.where(diagonal, 1.0, spacing)[:, None, :]
    )
    return jnp.prod(factors, axis=2)


def take_bit(number, position):
    return number >> position & 1


def phase_angles(
    step_index, box_code, target_bit, source_super, target_box, speed_rows, layout, child_bit
):
    across_boxes, down_boxes, tiles_across, tiles_down, supers_down = layout
    own_bit = level_bits[step_index]
    shift_across = merges_across[step_index]
    shift_down = merges_down[step_index]
    chosen = box_code & 15 - (1 << own_bit) | target_bit << own_bit
    whole_across = (
        4 * (source_super // supers_down) + 2 * take_bit(box_code, 1) + take_bit(box_code, 3)
    )
    whole_down = (
        4 * (source_super % supers_down) + 2 * take_bit(box_code, 0) + take_bit(box_code, 2)
    )
    side_across = 2**shift_across / across_boxes
    side_down = 2**shift_down / down_boxes
    corner_across = (whole_across >> shift_across).astype(jnp.float32) * side_across
    corner_down = (whole_down >> shift_down).astype(jnp.float32) * side_down
    tile_across = target_box // tiles_down * 2**shift_across + (
        2 * take_bit(chosen, 3) + take_bit(chosen, 1) >> 2 - shift_across
    )
    tile_down = target_box % tiles_down * 2**shift_down + (
        2 * take_bit(chosen, 2) + take_bit(chosen, 0) >> 2 - shift_down
    )
    center_across = (tile_across.astype(jnp.float32) + 0.5) / (tiles_across * 2**shift_across)
    center_down = (tile_down.astype(jnp.float32) + 0.5) / (tiles_down * 2**shift_down)
    node_set = cheb_nodes()
    along_first = node_set
    along_second = node_set
    if child_bit is not None:
        halved = (child_bit.astype(jnp.float32) + node_set) / 2.0
        if step_index % 2 == 0:
            along_first = halved
        else:
            along_second = halved
    key_across = corner_across[..., None, None] + side_across * along_first[:, None]
    key_down = corner_down[..., None, None] + side_down * along_second[None, :]
    base_across = (corner_across + 0.5 * side_across)[..., None, None]
    base_down = (corner_down + 0.5 * side_down)[..., None, None]
    key_square = key_across * key_across + key_down * key_down
    base_square = base_across * base_across + base_down * base_down
    radial = (key_square - base_square) / (jnp.sqrt(key_square) + jnp.sqrt(base_square))
    wave_scale = jnp.pi * across_boxes / 2.0
    return wave_scale * (
        center_across[..., None, None] * (key_across - base_across)
        + center_down[..., None, None] * (key_down - base_down)
        + speed_rows[..., None, None] * radial
    )


def pull_child(weights, angles, step_index, child_bit):
    shaped = weights.reshape(weights.shape[:-3] + (2, 8, 8, 16))
    real_part = shaped[..., 0, :, :, :]
    imag_part = shaped[..., 1, :, :, :]
    cosine = jnp.cos(angles)[..., None]
    sine_part = jnp.sin(angles)[..., None]
    turned_real = real_part * cosine + imag_part * sine_part
    turned_imag = imag_part * cosine - real_part * sine_part
    stacked = jnp.stack([turned_real, turned_imag], axis=-4)
    matrix = lagrange_matrix(child_bit)
    if step_index % 2 == 0:
        moved = jnp.einsum("ab,...bcd->...acd", matrix, stacked, precision=lax.Precision.HIGHEST)
    else:
        moved = jnp.einsum("ab,...cbd->...cad", matrix, stacked, precision=lax.Precision.HIGHEST)
    return moved.reshape(weights.shape)


def push_parent(summed, angles):
    shaped = summed.reshape(summed.shape[:-3] + (2, 8, 8, 16))
    real_part = shaped[..., 0, :, :, :]
    imag_part = shaped[..., 1, :, :, :]
    cosine = jnp.cos(angles)[..., None]
    sine_part = jnp.sin(angles)[..., None]
    out_real = real_part * cosine - imag_part * sine_part
    out_imag = real_part * sine_part + imag_part * cosine
    return jnp.stack([out_real, out_imag], axis=-4).reshape(summed.shape)


def merge_local(weights, step_index, code_base, source_super, target_box, speed_rows, layout):
    code_count = weights.shape[0]
    own_bit = level_bits[step_index]
    low_span = 1 << own_bit
    high_span = code_count // (2 * low_span)
    trailing = weights.shape[1:-3]
    split_view = weights.reshape((high_span, 2, low_span) + weights.shape[1:])
    ones_tail = (1,) * len(trailing)
    high_index = jnp.arange(high_span, dtype=jnp.int32).reshape((high_span, 1) + ones_tail)
    low_index = jnp.arange(low_span, dtype=jnp.int32).reshape((1, low_span) + ones_tail)
    results = []
    for target_bit in (0, 1):
        target_value = jnp.asarray(target_bit, dtype=jnp.int32)
        summed = None
        for child in (0, 1):
            child_value = jnp.asarray(child, dtype=jnp.int32)
            box_code = code_base + high_index * (2 * low_span) + child * low_span + low_index
            angles = phase_angles(
                step_index,
                box_code,
                target_value,
                source_super,
                target_box,
                speed_rows,
                layout,
                child_value,
            )
            term = pull_child(split_view[:, child], angles, step_index, child_value)
            summed = term if summed is None else summed + term
        parent_code = code_base + high_index * (2 * low_span) + low_index
        parent_angles = phase_angles(
            step_index,
            parent_code,
            target_value,
            source_super,
            target_box,
            speed_rows,
            layout,
            None,
        )
        results.append(push_parent(summed, parent_angles))
    return jnp.stack(results, axis=1).reshape(weights.shape)


def merge_partner(
    weights,
    step_index,
    box_code,
    code_base,
    source_super,
    target_box,
    speed_rows,
    layout,
    device_bit,
):
    own_bit = level_bits[step_index]
    child_bit = take_bit(code_base, own_bit)
    other_bit = 1 - child_bit
    outgoing = pull_child(
        weights,
        phase_angles(
            step_index, box_code, other_bit, source_super, target_box, speed_rows, layout, child_bit
        ),
        step_index,
        child_bit,
    )
    arrived = swapped(outgoing, "wide", device_bit)
    retained = pull_child(
        weights,
        phase_angles(
            step_index, box_code, child_bit, source_super, target_box, speed_rows, layout, child_bit
        ),
        step_index,
        child_bit,
    )
    parent_angles = phase_angles(
        step_index, box_code, child_bit, source_super, target_box, speed_rows, layout, None
    )
    return push_parent(retained + arrived, parent_angles)


def local(weights_in, medium_speed, target_order):
    narrow_count = lax.axis_size("narrow")
    layout = (8 * narrow_count, 4 * SYH, TX, TY, SYH)
    local_codes = weights_in.shape[0]
    per_super = weights_in.shape[1]
    tile_count = weights_in.shape[2]
    local_bits = local_codes.bit_length() - 1
    wide_place = lax.axis_index("wide")
    narrow_place = lax.axis_index("narrow")
    code_base = wide_place * local_codes
    speed_flat = medium_speed.reshape(-1)
    weights = weights_in
    source_super = (narrow_place * per_super + jnp.arange(per_super, dtype=jnp.int32))[:, None]
    target_box = jnp.arange(tile_count, dtype=jnp.int32)
    box_code = (code_base + jnp.arange(local_codes, dtype=jnp.int32))[:, None, None]
    for step_index in range(4):
        own_bit = level_bits[step_index]
        if own_bit < local_bits:
            weights = merge_local(
                weights, step_index, code_base, source_super, target_box, speed_flat, layout
            )
        else:
            weights = merge_partner(
                weights,
                step_index,
                box_code,
                code_base,
                source_super,
                target_box,
                speed_flat,
                layout,
                own_bit - local_bits,
            )
    ordered = jnp.swapaxes(jnp.take(weights, target_order, axis=2), 1, 2)
    return lax.all_to_all(ordered, "narrow", split_axis=1, concat_axis=2, tiled=True)


def solution(mesh):
    in_specs = (P("wide", "narrow", None, None, None, None), P(), P())
    out_specs = P("wide", "narrow", None, None, None, None)
    return jax.shard_map(local, mesh=mesh, in_specs=in_specs, out_specs=out_specs, check_vma=False)
```

profile of v0, /device:TPU:0, one launch (start us, length us, event | category | flops | bytes accessed | tf_op | source)
XLA Modules:
  0.0 1031.1 jit_solution(4115542343822853977)
XLA Ops:
  1.3 0.8 mul.2755
  2.1 12.2 %copy.222 = f32[2,8,64,2,8,128]{2,4,5,3,1,0:T(8,128)} copy(f32[2,8,64,2,8,128]{5,4,3,2,1,0:T(8,128)} %param.3) | data formatting | bytes 16777216 | tf_op args[0]
  15.1 7.0 fusion.61
  22.1 17.6 %multiply_add_fusion.7 = (f32[2,8,64,1,8,8,16]{2,4,6,5,3,1,0:T(8,128)}, f32[2,8,64,1,8,8,16]{2,4,6,5,3,1,0:T(8,128)}, f32[2,8,64,1,8,8,16]{2,4,6,5,3,1,0:T(8,128)}, f32[2,8,64,1,8,8,16]{2,4,6,5,3,1,0:T(8,128)}) fusion(f32[2,8,64,2,8,8,16]{2,4,6,5,3,1,0:T(8,128)} %bitcast.107, f32[2,8,64,8,8]{2,3,4,1,0:T(8,128)S(1)} %get-tuple-element.114, ...), kind=kLoop, calls=%fused_computation.64 | loop fusion | flops 12582912 | bytes 26214400 | tf_op jit(solution)/shard_map/add | solution.py:99
  39.7 1.2 fusion.101
  40.9 21.8 %fusion.4 = f32[2,8,64,2,8,16,8]{2,6,5,4,3,1,0:T(8,128)} fusion(f32[2,8,64,1,8,8,16]{2,4,6,5,3,1,0:T(8,128)} %get-tuple-element.43, f32[2,8,64,1,8,8,16]{2,4,6,5,3,1,0:T(8,128)} %get-tuple-element.42, f32[8,8]{1,0:T(8,128)S(1)} %get-tuple-element.9), kind=kOutput, calls=%fused_computation.5 | convolution fusion | flops 203423744 | bytes 16777472 | tf_op jit(solution)/shard_map/ab,...bcd->...acd/dot_general | solution.py:104
  62.7 13.1 %copy.224 = f32[2,8,64,2,8,128]{5,4,3,2,1,0:T(8,128)} copy(f32[2,8,64,2,8,128]{2,4,5,3,1,0:T(8,128)} %bitcast.105) | data formatting | bytes 16777216 | tf_op jit(solution)/shard_map/reshape | solution.py:107
  75.8 3.0 collective-permute-start
  78.8 21.5 %fusion = f32[2,8,64,2,8,16,8]{2,6,5,4,3,1,0:T(8,128)} fusion(f32[2,8,64,1,8,8,16]{2,4,6,5,3,1,0:T(8,128)} %get-tuple-element.52, f32[2,8,64,1,8,8,16]{2,4,6,5,3,1,0:T(8,128)} %get-tuple-element.53, f32[8,8]{1,0:T(8,128)S(1)} %get-tuple-element.9), kind=kOutput, calls=%fused_computation.1 | convolution fusion | flops 203423744 | bytes 16777472 | tf_op jit(solution)/shard_map/ab,...bcd->...acd/dot_general | solution.py:104
  100.3 13.0 %copy.225 = f32[2,8,64,2,8,128]{5,4,3,2,1,0:T(8,128)} copy(f32[2,8,64,2,8,128]{2,4,5,3,1,0:T(8,128)} %bitcast.103) | data formatting | bytes 16777216 | tf_op jit(solution)/shard_map/reshape | solution.py:107
  113.7 12.9 %fusion.50 = (f32[2,8,64,8,8]{2,3,4,1,0:T(8,128)}, f32[2,8,64,8,8]{2,3,4,1,0:T(8,128)}, f32[2,8,64,8,8]{2,3,4,1,0:T(8,128)S(1)}, f32[2,8,64,8,8]{2,3,4,1,0:T(8,1...) fusion(f32[2,8,8,8]{2,3,1,0:T(8,128)S(1)} %get-tuple-element.13, ...), kind=kLoop, calls=%fused_computation.95 | loop fusion | flops 1441792 | bytes 3490048 | tf_op jit(solution)/shard_map/cos | solution.py:114
  126.8 0.9 copy.228
  127.7 0.9 copy.230
  128.6 0.9 copy.231
  129.5 0.9 copy.232
  130.4 129.2 %collective-permute-done = f32[2,8,64,2,8,128]{5,4,3,2,1,0:T(8,128)} collective-permute-done((f32[2,8,64,2,8,128]{5,4,3,2,1,0:T(8,128)}, f32[2,8,64,2,8,128]{5,4,3,2,1,0:T(8,128)}, u32[]{:S(2)}, u32[]{:S(2)}) %collective-permute-start) | collective-permute-done | bytes 8388640 | tf_op jit(solution)/shard_map/ppermute | solution.py:19
  259.5 10.4 %add.3514 = f32[2,8,64,2,8,128]{5,4,3,2,1,0:T(8,128)} add(f32[2,8,64,2,8,128]{5,4,3,2,1,0:T(8,128)} %copy.225, f32[2,8,64,2,8,128]{5,4,3,2,1,0:T(8,128)} %collective-permute-done) | non-fusion elementwise | flops 2097152 | bytes 25165824 | tf_op jit(solution)/shard_map/add | solution.py:199
  270.0 12.6 %copy.226 = f32[2,8,64,2,8,128]{2,5,4,3,1,0:T(8,128)} copy(f32[2,8,64,2,8,128]{5,4,3,2,1,0:T(8,128)} %add.3514) | data formatting | bytes 16777216 | tf_op jit(solution)/shard_map/add | solution.py:199
  282.6 10.9 %fusion.144 = (f32[2,8,64,1,8,8,16]{2,6,5,4,3,1,0:T(8,128)}, f32[2,8,64,1,8,8,16]{2,6,5,4,3,1,0:T(8,128)}) fusion(f32[2,8,64,2,8,8,16]{2,6,5,4,3,1,0:T(8,128)} %bitcast.110), kind=kLoop, calls=%fused_computation.368 | loop fusion | bytes 16777216 | tf_op jit(solution)/shard_map/slice | solution.py:112
  293.4 19.4 %multiply_add_fusion.4 = (f32[2,8,64,1,8,8,16]{2,5,6,4,3,1,0:T(8,128)S(1)}, f32[2,8,64,1,8,8,16]{2,5,6,4,3,1,0:T(8,128)}, f32[2,8,64,1,8,8,16]{2,5,6,4,3,1,0:T(8,128)}) fusion(f32[2,8,64,8,8]{2,4,3,1,0:T(8,128)S(1)} %copy.235, f32[2,8,64,8,8]{2,4,3,1,0:T(8,128)S(1)} %copy.234, f32[2,8,64,8,8]{2,4,3,1,0:T(8,128)} %copy.228, ...), kind=kLoop, calls=%fused_computation.58 | loop fusion | flops 9437184 | bytes 22020096 | tf_op jit(solution)/shard_map/add | solution.py:99
  312.9 14.6 %multiply_add_fusion.5 = (f32[2,8,64,1,8,8,16]{2,5,6,4,3,1,0:T(8,128)}, f32[2,8,64,1,8,8,16]{2,5,6,4,3,1,0:T(8,128)}, f32[2,8,64,1,8,8,16]{2,5,6,4,3,1,0:T(8,128)}) fusion(f32[2,8,64,1,8,8,16]{2,5,6,4,3,1,0:T(8,128)} %get-tuple-element.27, f32[2,8,64,1,8,8,16]{2,5,6,4,3,1,0:T(8,128)} %get-tuple-element.28, f32[2,8,64,8,8]{2,4,3,1,0:T(8,128)} %copy.232, ...), kind=kLoop, calls=%fused_computation.60 | loop fusion | flops 9437184 | bytes 22020096 | tf_op jit(solution)/shard_map/add | solution.py:99
  327.5 18.3 %fusion.37 = f32[2,8,64,2,8,8,16]{2,5,6,4,3,1,0:T(8,128)} fusion(f32[2,8,64,1,8,8,16]{2,5,6,4,3,1,0:T(8,128)} %get-tuple-element.49, f32[2,8,64,1,8,8,16]{2,5,6,4,3,1,0:T(8,128)S(1)} %get-tuple-element.26, f32[8,8]{1,0:T(8,128)S(1)} %get-tuple-element.6), kind=kOutput, calls=%fused_computation.67 | convolution fusion | flops 203423744 | bytes 16777472 | tf_op jit(solution)/shard_map/ab,...cbd->...cad/dot_general | solution.py:106
  345.8 14.1 %copy.236 = f32[2,8,64,2,8,8,16]{2,6,5,4,3,1,0:T(8,128)} copy(f32[2,8,64,2,8,8,16]{2,5,6,4,3,1,0:T(8,128)} %fusion.37) | data formatting | bytes 16777216 | tf_op jit(solution)/shard_map/ab,...cbd->...cad/transpose | solution.py:106
  359.9 12.8 %copy.237 = f32[2,8,64,2,8,128]{5,4,3,2,1,0:T(8,128)} copy(f32[2,8,64,2,8,128]{2,5,4,3,1,0:T(8,128)} %bitcast.111) | data formatting | bytes 16777216 | tf_op jit(solution)/shard_map/reshape | solution.py:107
  372.7 1.7 collective-permute-start.1
  374.5 21.5 %fusion.40 = f32[2,8,64,2,8,8,16]{2,5,6,4,3,1,0:T(8,128)} fusion(f32[2,8,64,1,8,8,16]{2,5,6,4,3,1,0:T(8,128)} %get-tuple-element.41, f32[2,8,64,1,8,8,16]{2,5,6,4,3,1,0:T(8,128)} %get-tuple-element.40, f32[8,8]{1,0:T(8,128)S(1)} %get-tuple-element.6), kind=kOutput, calls=%fused_computation.68 | convolution fusion | flops 203423744 | bytes 16777472 | tf_op jit(solution)/shard_map/ab,...cbd->...cad/dot_general | solution.py:106
  395.9 14.1 %copy.233 = f32[2,8,64,2,8,8,16]{2,6,5,4,3,1,0:T(8,128)} copy(f32[2,8,64,2,8,8,16]{2,5,6,4,3,1,0:T(8,128)} %fusion.40) | data formatting | bytes 16777216 | tf_op jit(solution)/shard_map/ab,...cbd->...cad/transpose | solution.py:106
  410.0 12.8 %copy.238 = f32[2,8,64,2,8,128]{5,4,3,2,1,0:T(8,128)} copy(f32[2,8,64,2,8,128]{2,5,4,3,1,0:T(8,128)} %bitcast.112) | data formatting | bytes 16777216 | tf_op jit(solution)/shard_map/reshape | solution.py:107
  422.9 131.8 %collective-permute-done.1 = f32[2,8,64,2,8,128]{5,4,3,2,1,0:T(8,128)} collective-permute-done((f32[2,8,64,2,8,128]{5,4,3,2,1,0:T(8,128)}, f32[2,8,64,2,8,128]{5,4,3,2,1,0:T(8,128)}, u32[]{:S(2)}, u32[]{:S(2)}) %collective-permute-start.1) | collective-permute-done | bytes 8388640 | tf_op jit(solution)/shard_map/ppermute | solution.py:19
  554.7 10.4 %add.3561 = f32[2,8,64,2,8,128]{5,4,3,2,1,0:T(8,128)} add(f32[2,8,64,2,8,128]{5,4,3,2,1,0:T(8,128)} %copy.238, f32[2,8,64,2,8,128]{5,4,3,2,1,0:T(8,128)} %collective-permute-done.1) | non-fusion elementwise | flops 2097152 | bytes 25165824 | tf_op jit(solution)/shard_map/add | solution.py:199
  565.1 12.3 %copy.271 = f32[2,8,64,2,8,128]{2,4,5,3,1,0:T(8,128)} copy(f32[2,8,64,2,8,128]{5,4,3,2,1,0:T(8,128)} %add.3561) | data formatting | bytes 16777216 | tf_op jit(solution)/shard_map/reshape | solution.py:111
  577.4 12.0 %multiply_add_fusion.1 = (f32[2,8,64,1,8,8,16]{2,4,6,5,3,1,0:T(8,128)S(1)}, f32[2,8,64,1,8,8,16]{2,4,6,5,3,1,0:T(8,128)}, f32[2,8,64,1,8,8,16]{2,4,6,5,3,1,0:T(8,128)}) fusion(f32[2,8,64,8,8]{2,3,4,1,0:T(8,128)S(1)} %get-tuple-element.106, f32[2,8,64,8,8]{2,3,4,1,0:T(8,128)S(1)} %get-tuple-element.107, f32[2,8,64,8,8]{2,3,4,1,0:T(8,128)S(1)} %copy-done.3, ...), kind=kLoop, calls=%fused_computation.52 | loop fusion | flops 9437184 | bytes 22020096 | tf_op jit(solution)/shard_map/add | solution.py:99
  589.4 14.9 %multiply_add_fusion.2 = (f32[2,8,64,1,8,8,16]{2,4,6,5,3,1,0:T(8,128)}, f32[2,8,64,1,8,8,16]{2,4,6,5,3,1,0:T(8,128)}, f32[2,8,64,1,8,8,16]{2,4,6,5,3,1,0:T(8,128)}) fusion(f32[2,8,64,1,8,8,16]{2,4,6,5,3,1,0:T(8,128)} %get-tuple-element.19, f32[2,8,64,1,8,8,16]{2,4,6,5,3,1,0:T(8,128)} %get-tuple-element.20, f32[2,8,64,8,8]{2,3,4,1,0:T(8,128)S(1)} %get-tuple-element.104, ...), kind=kLoop, calls=%fused_computation.54 | loop fusion | flops 9437184 | bytes 22020096 | tf_op jit(solution)/shard_map/add | solution.py:99
  604.3 18.3 %fusion.20 = f32[2,8,64,2,8,16,8]{2,6,5,4,3,1,0:T(8,128)} fusion(f32[2,8,64,1,8,8,16]{2,4,6,5,3,1,0:T(8,128)} %get-tuple-element.48, f32[2,8,64,1,8,8,16]{2,4,6,5,3,1,0:T(8,128)S(1)} %get-tuple-element.18, f32[8,8]{1,0:T(8,128)S(1)} %copy-done.9), kind=kOutput, calls=%fused_computation.21 | convolution fusion | flops 203423744 | bytes 16777472 | tf_op jit(solution)/shard_map/ab,...bcd->...acd/dot_general | solution.py:104
  622.7 13.1 %copy.243 = f32[2,8,64,2,8,128]{5,4,3,2,1,0:T(8,128)} copy(f32[2,8,64,2,8,128]{2,4,5,3,1,0:T(8,128)} %bitcast.106) | data formatting | bytes 16777216 | tf_op jit(solution)/shard_map/reshape | solution.py:107
  636.9 7.0 fusion.80
  644.0 21.8 %fusion.16 = f32[2,8,64,2,8,16,8]{2,6,5,4,3,1,0:T(8,128)} fusion(f32[2,8,64,1,8,8,16]{2,4,6,5,3,1,0:T(8,128)} %get-tuple-element.39, f32[2,8,64,1,8,8,16]{2,4,6,5,3,1,0:T(8,128)} %get-tuple-element.38, f32[8,8]{1,0:T(8,128)S(1)} %copy-done.9), kind=kOutput, calls=%fused_computation.17 | convolution fusion | flops 203423744 | bytes 16777472 | tf_op jit(solution)/shard_map/ab,...bcd->...acd/dot_general | solution.py:104
  665.7 13.0 %copy.244 = f32[2,8,64,2,8,128]{5,4,3,2,1,0:T(8,128)} copy(f32[2,8,64,2,8,128]{2,4,5,3,1,0:T(8,128)} %bitcast.104) | data formatting | bytes 16777216 | tf_op jit(solution)/shard_map/reshape | solution.py:107
  678.7 10.4 %add.3609 = f32[2,8,64,2,8,128]{5,4,3,2,1,0:T(8,128)} add(f32[2,8,64,2,8,128]{5,4,3,2,1,0:T(8,128)} %copy.244, f32[2,8,64,2,8,128]{5,4,3,2,1,0:T(8,128)} %collective-permute-done.2) | non-fusion elementwise | flops 2097152 | bytes 25165824 | tf_op jit(solution)/shard_map/add | solution.py:199
  689.1 12.2 %copy.245 = f32[2,8,64,2,8,128]{2,5,4,3,1,0:T(8,128)} copy(f32[2,8,64,2,8,128]{5,4,3,2,1,0:T(8,128)} %add.3609) | data formatting | bytes 16777216 | tf_op jit(solution)/shard_map/add | solution.py:199
  701.3 11.5 %multiply_add_fusion = (f32[2,8,64,1,8,8,16]{2,6,5,4,3,1,0:T(8,128)}, f32[2,8,64,1,8,8,16]{2,6,5,4,3,1,0:T(8,128)}) fusion(f32[2,8,64,2,8,8,16]{2,6,5,4,3,1,0:T(8,128)} %bitcast.109, f32[2,8,64,8,8]{2,4,3,1,0:T(8,128)S(1)} %copy.247, f32[2,8,64,8,8]{2,4,3,1,0:T(8,128)S(1)} %copy.246), kind=kLoop, calls=%fused_computation.49 | loop fusion | flops 6291456 | bytes 17301504 | tf_op jit(solution)/shard_map/add | solution.py:117
  712.8 6.9 pad_maximum_fusion
  719.7 4.1 fusion.146
  724.4 10.3 multiply_add_fusion.14
  734.7 7.3 fusion.25
  742.0 9.6 multiply_add_fusion.13
  751.7 10.1 add_bitcast_fusion.1
  761.7 4.1 multiply_subtract_fusion.12
  765.8 2.9 copy.254
  768.7 3.5 copy.256
  772.3 5.1 copy.255
  777.4 4.2 copy.257
  781.6 10.0 fusion.31
  791.6 7.4 add_bitcast_fusion
  798.9 5.1 multiply_subtract_fusion.9
  804.1 2.9 copy.258
  807.0 4.2 copy.260
  811.2 5.1 copy.259
  816.3 4.4 copy.261
  820.7 5.7 maximum_bitcast_fusion.8
  826.4 7.8 gather_fusion
  834.1 4.5 select_bitcast_fusion
  838.6 188.3 %all_to_all.18 = f32[2,64,8,2,8,128]{5,4,3,2,0,1:T(8,128)S(1)} all-to-all(f32[2,64,8,2,8,128]{5,4,3,2,0,1:T(8,128)S(1)} %select_bitcast_fusion), channel_id=1, replica_groups=mesh['wide'=8,'narrow'=4] {'narrow'}, dimensions={1} | all-to-all | bytes 16777216 | tf_op jit(solution)/shard_map/all_to_all | solution.py:236
  1026.9 4.0 copy.263
  (99 shorter events, 4.3 us)
Async XLA Ops:
  0.7 13.9 %copy-start.13 = (f32[8]{0:T(128)}, f32[8]{0:T(128)S(1)}, u32[]{:S(2)}) copy-start(f32[8]{0:T(128)S(1)} %get-tuple-element.268) | copy-start | bytes 100
  2.1 111.5 %copy-start.11 = (f32[64]{0:T(128)}, f32[64]{0:T(128)S(1)}, u32[]{:S(2)}) copy-start(f32[64]{0:T(128)S(1)} %mul.2755) | copy-start | bytes 772
  75.8 183.7 %collective-permute-start = (f32[2,8,64,2,8,128]{5,4,3,2,1,0:T(8,128)}, f32[2,8,64,2,8,128]{5,4,3,2,1,0:T(8,128)}, u32[]{:S(2)}, u32[]{:S(2)}) collective-permute-start(f32[2,8,64,2,8,128]{5,4,3,2,1,0:T(8,128)} %copy.224), channel_id=1, source_target_pairs={{0,16},{4,20},{8,24},{12,28},{16,0},{20,4},{24,8},{28,12},{1,17},{... | collective-permute-start | bytes 25165832 | tf_op jit(solution)/shard_map/ppermute | solution.py:19
  113.2 13.6 %copy-start.7 = (f32[2,8,64,8,8]{2,3,4,1,0:T(8,128)S(1)}, f32[2,8,64,8,8]{2,3,4,1,0:T(8,128)}, u32[]{:S(2)}) copy-start(f32[2,8,64,8,8]{2,3,4,1,0:T(8,128)} %get-tuple-element.83) | copy-start | bytes 786436
  113.2 14.5 %copy-start.6 = (f32[2,8,64,8,8]{2,3,4,1,0:T(8,128)S(1)}, f32[2,8,64,8,8]{2,3,4,1,0:T(8,128)}, u32[]{:S(2)}) copy-start(f32[2,8,64,8,8]{2,3,4,1,0:T(8,128)} %get-tuple-element.82) | copy-start | bytes 786436
  372.7 182.0 %collective-permute-start.1 = (f32[2,8,64,2,8,128]{5,4,3,2,1,0:T(8,128)}, f32[2,8,64,2,8,128]{5,4,3,2,1,0:T(8,128)}, u32[]{:S(2)}, u32[]{:S(2)}) collective-permute-start(f32[2,8,64,2,8,128]{5,4,3,2,1,0:T(8,128)} %copy.237), channel_id=1, source_target_pairs={{0,8},{4,12},{8,0},{12,4},{16,24},{20,28},{24,16},{28,20},{1,9},{5... | collective-permute-start | bytes 25165832 | tf_op jit(solution)/shard_map/ppermute | solution.py:19
  565.1 12.3 %copy-start.3 = (f32[2,8,64,8,8]{2,3,4,1,0:T(8,128)S(1)}, f32[2,8,64,8,8]{2,3,4,1,0:T(8,128)}, u32[]{:S(2)}) copy-start(f32[2,8,64,8,8]{2,3,4,1,0:T(8,128)} %get-tuple-element.217) | copy-start | bytes 786436
  577.4 12.0 %copy-start.2 = (f32[2,8,64,8,8]{2,3,4,1,0:T(8,128)S(1)}, f32[2,8,64,8,8]{2,3,4,1,0:T(8,128)}, u32[]{:S(2)}) copy-start(f32[2,8,64,8,8]{2,3,4,1,0:T(8,128)} %get-tuple-element.105) | copy-start | bytes 786436
  589.4 14.9 %copy-start.9 = (f32[8,8]{1,0:T(8,128)S(1)}, f32[8,8]{1,0:T(8,128)}, u32[]{:S(2)}) copy-start(f32[8,8]{1,0:T(8,128)} %get-tuple-element.7) | copy-start | bytes 772
  622.6 13.1 %copy-start.5 = (f32[2,8,64,8,8]{2,3,4,1,0:T(8,128)S(1)}, f32[2,8,64,8,8]{2,3,4,1,0:T(8,128)}, u32[]{:S(2)}) copy-start(f32[2,8,64,8,8]{2,3,4,1,0:T(8,128)} %get-tuple-element.74) | copy-start | bytes 786436
  622.6 13.2 %copy-start.4 = (f32[2,8,64,8,8]{2,3,4,1,0:T(8,128)S(1)}, f32[2,8,64,8,8]{2,3,4,1,0:T(8,128)}, u32[]{:S(2)}) copy-start(f32[2,8,64,8,8]{2,3,4,1,0:T(8,128)} %get-tuple-element.75) | copy-start | bytes 786436
  622.6 13.5 %copy-start.16 = (s32[64]{0:T(128)S(1)}, s32[64]{0:T(128)}, u32[]{:S(2)}) copy-start(s32[64]{0:T(128)} %param.5) | copy-start | bytes 772
  622.6 13.7 %copy-start.14 = (f32[8]{0:T(128)S(1)}, f32[8]{0:T(128)}, u32[]{:S(2)}) copy-start(f32[8]{0:T(128)} %copy-done.13) | copy-start | bytes 100
  622.6 13.7 %copy-start.15 = (f32[8]{0:T(128)S(1)}, f32[8]{0:T(128)}, u32[]{:S(2)}) copy-start(f32[8]{0:T(128)} %get-tuple-element.267) | copy-start | bytes 100
  622.7 14.3 %copy-start.12 = (f32[64]{0:T(128)S(1)}, f32[64]{0:T(128)}, u32[]{:S(2)}) copy-start(f32[64]{0:T(128)} %copy-done.11) | copy-start | bytes 772
  635.7 43.0 %collective-permute-start.2 = (f32[2,8,64,2,8,128]{5,4,3,2,1,0:T(8,128)}, f32[2,8,64,2,8,128]{5,4,3,2,1,0:T(8,128)}, u32[]{:S(2)}, u32[]{:S(2)}) collective-permute-start(f32[2,8,64,2,8,128]{5,4,3,2,1,0:T(8,128)} %copy.243), channel_id=1, source_target_pairs={{0,4},{4,0},{8,12},{12,8},{16,20},{20,16},{24,28},{28,24},{1,5},{5... | collective-permute-start | bytes 25165832 | tf_op jit(solution)/shard_map/ppermute | solution.py:19
  724.4 10.3 copy-start.8
  742.0 9.6 copy-start.10
  781.6 10.0 copy-start
  781.6 10.0 copy-start.1
where the time goes:
time: 1040 us; the launch traced here: 1030 us
  waiting for transfers between devices  261 us (25%)
  local copies, waits for them, and re-layouts  220 us (21%)
  other arithmetic  199 us (19%)
  blocking collectives  188 us (18%)
  matrix products  158 us (15%)
    ppermute x3, waiting for transfers between devices, swapped(): return lax.ppermute(value, axis, pairs)  261 us
    all_to_all x1, blocking collectives, local(): lax.all_to_all(ordered, 'narrow', split_axis=1, concat_axis=2, tiled=True)  188 us
    add x7, other arithmetic, pull_child(): turned_real = real_part * cosine + imag_part * sine_part  98.4 us
    dot_general x4, matrix products, pull_child(): jnp.einsum('ab,...bcd->...acd', matrix, stacked, precision=lax.Precision....  83.4 us
    reshape x6, local copies, waits for them, and re-layouts, pull_child(): return moved.reshape(weights.shape)  77.7 us
    dot_general x6, matrix products, pull_child(): jnp.einsum('ab,...cbd->...cad', matrix, stacked, precision=lax.Precision....  74.5 us
    add x3, other arithmetic, merge_partner(): return push_parent(retained + arrived, parent_angles)  31.2 us
    transpose x2, local copies, waits for them, and re-layouts, pull_child(): jnp.einsum('ab,...cbd->...cad', matrix, stacked, precision=lax.Precision....  28.2 us
  transfers between devices with their start and end apart: 3, of which 2 were waited for; matrix products, arithmetic and copies ran while one was open for 14% of the time, Pallas kernels for 0%

commit v1 on v0

v1 whole, which is shorter than its diff:
```python
import functools

import jax
import jax.numpy as jnp
import ml_dtypes
import numpy as np
from jax import lax
from jax.experimental import pallas as pl
from jax.experimental.pallas import tpu as pltpu
from jax.sharding import PartitionSpec as P

TX = 8
TY = 8
SYH = 4
SUPERS = 4

MESH = pl.DeviceIdType.MESH
level_bits = (3, 2, 1, 0)


def cheb_nodes():
    return 0.5 - 0.5 * np.cos(np.pi * (2.0 * np.arange(8) + 1.0) / 16.0)


def lagrange_matrix(child):
    nodes = cheb_nodes()
    points = (child + nodes) / 2.0
    matrix = np.ones((8, 8))
    for q in range(8):
        for m in range(8):
            if m != q:
                matrix[q] *= (points - nodes[m]) / (nodes[q] - nodes[m])
    return matrix


def level_matrix(level, across_boxes, high, target, child):
    nodes = cheb_nodes()
    merges = 1 + level // 2
    boxes = across_boxes if level % 2 == 0 else 4 * SYH
    tiles = TX if level % 2 == 0 else TY
    side = 2.0**merges / boxes
    if merges == 1:
        shift = (target - 0.5) / (2 * tiles)
    else:
        shift = (2 * high + target - 1.5) / (4 * tiles)
    wave = np.pi * across_boxes / 2.0 * shift * side
    parent = np.exp(1j * wave * (nodes - 0.5))
    inner = np.exp(-1j * wave * ((child + nodes) / 2.0 - 0.5))
    matrix = parent[:, None] * lagrange_matrix(child) * inner[None, :]
    return np.block([[matrix.real, -matrix.imag], [matrix.imag, matrix.real]])


def all_matrices(across_boxes):
    found = []
    for level in range(4):
        for high in range(1 if level < 2 else 2):
            for target in range(2):
                for child in range(2):
                    small = level_matrix(level, across_boxes, high, target, child)
                    if level % 2 == 0:
                        big = np.kron(np.eye(16), small)
                    else:
                        big = np.kron(small.T, np.eye(16))
                    first = big.astype(np.float32).astype(ml_dtypes.bfloat16)
                    rest = (big - first.astype(np.float64)).astype(np.float32)
                    found.append(np.stack([first, rest.astype(ml_dtypes.bfloat16)]))
    return np.stack(found)


def turned(turns):
    part = turns - jnp.floor(turns + 0.5)
    half = part * np.float32(np.pi)
    square = half * half
    sine = np.float32(-1.0 / 39916800.0)
    for value in (1.0 / 362880.0, -1.0 / 5040.0, 1.0 / 120.0, -1.0 / 6.0, 1.0):
        sine = sine * square + np.float32(value)
    sine = sine * half
    cosine = np.float32(1.0 / 479001600.0)
    for value in (-1.0 / 3628800.0, 1.0 / 40320.0, -1.0 / 720.0, 1.0 / 24.0, -0.5, 1.0):
        cosine = cosine * square + np.float32(value)
    return 1.0 - 2.0 * sine * sine, 2.0 * sine * cosine


def split_two(value):
    first = value.astype(jnp.bfloat16)
    return first, (value - first.astype(jnp.float32)).astype(jnp.bfloat16)


def dot(left, right):
    return jnp.dot(left, right, preferred_element_type=jnp.float32)


def kernel(
    sizes,
    order_ref,
    speed_ref,
    weights_ref,
    mats_ref,
    nodes_ref,
    out_ref,
    held,
    outgoing,
    arrived,
    send_sem,
    recv_sem,
    far_send,
    far_recv,
    own_sem,
):
    wide, narrow, codes, supers, slots = sizes
    partner_levels = wide.bit_length() - 1
    local_bits = codes.bit_length() - 1
    parts = supers // SUPERS
    chunks = slots * parts
    across_boxes = 8 * narrow
    boxes = narrow * codes * SUPERS
    wide_place = lax.axis_index("wide")
    narrow_place = lax.axis_index("narrow")

    def device_bit(level):
        return wide_place >> (level_bits[level] - local_bits) & 1

    def partner(level):
        step = 1 << (level_bits[level] - local_bits)
        return wide_place + step * (1 - 2 * device_bit(level))

    def matrix(level, target, child):
        if level < 2:
            place = 4 * level + 2 * target + child
        else:
            place = 8 * level - 8 + 4 * device_bit(level - 2) + 2 * target + child
        return mats_ref[place, 0], mats_ref[place, 1]

    def far(step):
        return lax.rem(narrow_place + step, narrow)

    barrier = pltpu.get_barrier_semaphore()
    for level in range(partner_levels):
        pl.semaphore_signal(
            barrier, inc=1, device_id={"wide": partner(level)}, device_id_type=MESH
        )
    for step in range(1, narrow):
        pl.semaphore_signal(barrier, inc=1, device_id={"narrow": far(step)}, device_id_type=MESH)
    pl.semaphore_wait(barrier, partner_levels + narrow - 1)

    def swap(level, k):
        return pltpu.make_async_remote_copy(
            src_ref=outgoing.at[k],
            dst_ref=arrived.at[level, k],
            send_sem=send_sem.at[level, k],
            recv_sem=recv_sem.at[level, k],
            device_id={"wide": partner(level)},
            device_id_type=MESH,
        )

    def place_of(k):
        return out_ref.at[
            :, k // parts, pl.ds(narrow_place * supers + lax.rem(k, parts) * SUPERS, SUPERS)
        ]

    def hand_over(step, k):
        return pltpu.make_async_remote_copy(
            src_ref=outgoing.at[k, far(step)],
            dst_ref=place_of(k),
            send_sem=far_send.at[step - 1, k],
            recv_sem=far_recv.at[step - 1, k],
            device_id={"narrow": far(step)},
            device_id_type=MESH,
        )

    def hand_own(k):
        return pltpu.make_async_copy(outgoing.at[k, narrow_place], place_of(k), own_sem.at[k])

    def target_of(slot):
        box = order_ref[slot]
        speed = speed_ref[box]
        center_across = ((box // TY).astype(jnp.float32) + 0.5) * np.float32(1.0 / TX)
        center_down = ((box % TY).astype(jnp.float32) + 0.5) * np.float32(1.0 / TY)
        return box, center_across, center_down, speed * np.float32(across_boxes / 4.0)

    def radial(k, index, offset_across, offset_down):
        place = narrow_place * supers + lax.rem(k, parts) * SUPERS + index
        corner_across = (4 * (place // SYH)).astype(jnp.float32)
        corner_down = (4 * (place % SYH)).astype(jnp.float32)
        unit_across = np.float32(1.0 / across_boxes)
        unit_down = np.float32(1.0 / (4 * SYH))
        first = (corner_across + offset_across) * unit_across
        second = (corner_down + offset_down) * unit_down
        base_first = jnp.full((8, 128), (corner_across + 2.0) * unit_across)
        base_second = jnp.full((8, 128), (corner_down + 2.0) * unit_down)
        square = first * first + second * second
        base = base_first * base_first + base_second * base_second
        return (square - base) / (jnp.sqrt(square) + jnp.sqrt(base))

    nodes_across = nodes_ref[0]
    nodes_down = nodes_ref[1]
    down_scale = np.float32(across_boxes / 4.0 / (4 * SYH))

    def along_first(value):
        rows = value.reshape(boxes * 16, 128)
        pieces = [rows[256 * n : 256 * n + 256] for n in range(boxes // 16)]
        return split_two(jnp.concatenate(pieces, axis=1))

    def first_product(split, pair):
        total = dot(pair[0], split[0]) + dot(pair[0], split[1]) + dot(pair[1], split[0])
        pieces = [total[:, 128 * n : 128 * n + 128] for n in range(boxes // 16)]
        return jnp.concatenate(pieces, axis=0).reshape(narrow, codes, SUPERS, 2, 8, 128)

    def along_second(value):
        count = value.shape[0] * value.shape[1] * value.shape[2] * 8
        real = value[:, :, :, 0].reshape(count, 128)
        imag = value[:, :, :, 1].reshape(count, 128)
        return split_two(jnp.concatenate([real, imag], axis=1))

    def second_product(split, pair):
        return dot(split[0], pair[0]) + dot(split[1], pair[0]) + dot(split[0], pair[1])

    def store(into, level, k, split, pair):
        if level % 2 == 0:
            into[k] = first_product(split, pair)
        else:
            total = second_product(split, pair)
            shape = (narrow, codes, SUPERS, 8, 128)
            into[k, :, :, :, 0] = total[:, :128].reshape(shape)
            into[k, :, :, :, 1] = total[:, 128:].reshape(shape)

    def exchange(level, k, value):
        bit = device_bit(level)
        split = along_first(value) if level % 2 == 0 else along_second(value)
        store(outgoing, level, k, split, matrix(level, 1 - bit, bit))
        swap(level, k).start()
        store(held, level, k, split, matrix(level, bit, bit))

    def enter(k):
        base_super = lax.rem(k, parts) * SUPERS
        targets = [target_of(z * slots + k // parts) for z in range(narrow)]
        for code in range(codes):
            whole = wide_place * codes + code
            add_across = (2 * (whole >> 1 & 1) + (whole >> 3 & 1)).astype(jnp.float32)
            add_down = (2 * (whole & 1) + (whole >> 2 & 1)).astype(jnp.float32)
            offset_across = nodes_across + add_across
            offset_down = nodes_down + add_down
            across = (offset_across - 2.0) * 0.25
            down = (offset_down - 2.0) * down_scale
            for index in range(SUPERS):
                lengths = radial(k, index, offset_across, offset_down)
                for z, (box, center_across, center_down, speed) in enumerate(targets):
                    cosine, sine = turned(
                        center_across * across + center_down * down + speed * lengths
                    )
                    real = weights_ref[code, base_super + index, box, 0]
                    imag = weights_ref[code, base_super + index, box, 1]
                    held[k, z, code, index, 0] = real * cosine + imag * sine
                    held[k, z, code, index, 1] = imag * cosine - real * sine
        exchange(0, k, held[k])

    def middle(level, k):
        swap(level - 1, k).wait()
        exchange(level, k, held[k] + arrived[level - 1, k])

    def leave(k):
        swap(partner_levels - 1, k).wait()
        value = held[k] + arrived[partner_levels - 1, k]
        results = []
        if partner_levels == 4:
            results.append((value[:, 0, :, 0], value[:, 0, :, 1]))
        else:
            splits = [along_second(value[:, child : child + 1]) for child in range(2)]
            for target in range(2):
                total = second_product(splits[0], matrix(3, target, 0))
                total = total + second_product(splits[1], matrix(3, target, 1))
                shape = (narrow, SUPERS, 8, 128)
                results.append((total[:, :128].reshape(shape), total[:, 128:].reshape(shape)))
        targets = [target_of(z * slots + k // parts) for z in range(narrow)]
        across = nodes_across - 0.5
        down = (4.0 * nodes_down - 2.0) * down_scale
        for index in range(SUPERS):
            lengths = radial(k, index, 4.0 * nodes_across, 4.0 * nodes_down)
            for z, (_, center_across, center_down, speed) in enumerate(targets):
                cosine, sine = turned(
                    center_across * across + center_down * down + speed * lengths
                )
                for code, (real, imag) in enumerate(results):
                    real, imag = real[z, index], imag[z, index]
                    outgoing[k, z, code, index, 0] = real * cosine - imag * sine
                    outgoing[k, z, code, index, 1] = real * sine + imag * cosine
        for step in range(1, narrow):
            hand_over(step, k).start()
        hand_own(k).start()

    stages = [(0, enter)]
    for level in range(1, partner_levels):
        stages.append((2 * level, functools.partial(middle, level)))
    stages.append((2 * partner_levels - 1, leave))

    def turn(now, carry):
        for lag, stage in stages:
            k = now - lag
            pl.when((k >= 0) & (k < chunks))(functools.partial(stage, k))
        return carry

    lax.fori_loop(0, chunks + stages[-1][0], turn, 0)

    def finish(k, carry):
        for step in range(1, narrow):
            hand_over(step, k).wait()
        hand_own(k).wait()
        return carry

    lax.fori_loop(0, chunks, finish, 0)


def local(weights_in, medium_speed, target_order):
    wide = lax.axis_size("wide")
    narrow = lax.axis_size("narrow")
    codes, supers, tiles = weights_in.shape[:3]
    slots = tiles // narrow
    chunks = slots * (supers // SUPERS)
    partner_levels = wide.bit_length() - 1
    nodes = cheb_nodes().astype(np.float32)
    node_table = np.stack(
        [np.repeat(nodes[:, None], 128, axis=1), np.repeat(np.repeat(nodes, 16)[None], 8, axis=0)]
    )
    chunk_shape = (narrow, codes, SUPERS, 2, 8, 128)
    sizes = (wide, narrow, codes, supers, slots)
    scalars = pl.BlockSpec(memory_space=pltpu.SMEM)
    vectors = pl.BlockSpec(memory_space=pltpu.VMEM)
    return pl.pallas_call(
        functools.partial(kernel, sizes),
        out_shape=jax.ShapeDtypeStruct(
            (codes, slots, supers * narrow) + weights_in.shape[3:], jnp.float32
        ),
        in_specs=[scalars, scalars, vectors, vectors, vectors],
        out_specs=pl.BlockSpec(memory_space=pl.ANY),
        scratch_shapes=[
            pltpu.VMEM((chunks,) + chunk_shape, jnp.float32),
            pltpu.VMEM((chunks,) + chunk_shape, jnp.float32),
            pltpu.VMEM((partner_levels, chunks) + chunk_shape, jnp.float32),
            pltpu.SemaphoreType.DMA((partner_levels, chunks)),
            pltpu.SemaphoreType.DMA((partner_levels, chunks)),
            pltpu.SemaphoreType.DMA((narrow - 1, chunks)),
            pltpu.SemaphoreType.DMA((narrow - 1, chunks)),
            pltpu.SemaphoreType.DMA((chunks,)),
        ],
        compiler_params=pltpu.CompilerParams(
            collective_id=0, has_side_effects=True, vmem_limit_bytes=62 * 2**20
        ),
    )(
        target_order,
        medium_speed.reshape(-1),
        weights_in,
        jnp.asarray(all_matrices(8 * narrow)),
        jnp.asarray(node_table),
    )


def solution(mesh):
    in_specs = (P("wide", "narrow", None, None, None, None), P(), P())
    out_specs = P("wide", "narrow", None, None, None, None)
    return jax.shard_map(local, mesh=mesh, in_specs=in_specs, out_specs=out_specs, check_vma=False)
```

time: 1040 us -> 230 us (0.22)
  waiting for transfers between devices: 261 us -> 0 us
  Pallas kernels: 0 us -> 220 us
  local copies, waits for them, and re-layouts: 220 us -> 8.93 us
  other arithmetic: 199 us -> 0 us
  blocking collectives: 188 us -> 0 us
  matrix products: 158 us -> 0 us
    ppermute x3 -> x0, waiting for transfers between devices: 261 us -> none  [swapped(): return lax.ppermute(value, axis, pairs)]
    pallas_call x0 -> x1, Pallas kernels: none -> 220 us  [local(): pl.pallas_call(functools.partial(kernel, sizes), out_shape=jax.ShapeDtype...]
    all_to_all x1 -> x0, blocking collectives: 188 us -> none  [local(): lax.all_to_all(ordered, 'narrow', split_axis=1, concat_axis=2, tiled=True)]
    dot_general x10 -> x0, matrix products: 158 us -> none  [the longest x4 83.4 us: pull_child(): jnp.einsum('ab,...bcd->...acd', matrix, stacked, precision=lax.Precision....]
    add x17 -> x0, other arithmetic: 141 us -> none  [the longest x7 98.4 us: pull_child(): turned_real = real_part * cosine + imag_part * sine_part]
    reshape x7 -> x1, local copies, waits for them, and re-layouts: 90 us -> 1.28 us  [local(): medium_speed.reshape(-1)]
    add x4 -> x0, local copies, waits for them, and re-layouts: 35 us -> none  [the longest x2 24.8 us: merge_partner(): return push_parent(retained + arrived, parent_angles)]
    transpose x2 -> x0, local copies, waits for them, and re-layouts: 28.2 us -> none  [pull_child(): jnp.einsum('ab,...cbd->...cad', matrix, stacked, precision=lax.Precision....]
  transfers between devices with their start and end apart: 3 -> 0, of which waited for: 2 -> 0; matrix products, arithmetic and copies ran while one was open for 14% -> 0% of each run, Pallas kernels for 0% -> 0%
where the time goes in v1:
time: 230 us; the launch traced here: 229 us
  Pallas kernels  220 us (96%)
  local copies, waits for them, and re-layouts  8.93 us (4%)
    pallas_call x1, Pallas kernels, local(): pl.pallas_call(functools.partial(kernel, sizes), out_shape=jax.ShapeDtype...  220 us
    unnamed x1, local copies, waits for them, and re-layouts  7.65 us

profile of v1, /device:TPU:0, one launch (start us, length us, event | category | flops | bytes accessed | tf_op | source)
XLA Modules:
  0.0 229.4 jit_solution(12600337820543133302)
XLA Ops:
  0.0 1.3 reshape.3.speed_ref
  1.3 220.4 %shard_map.55 = f32[2,16,32,2,8,128]{5,4,3,2,1,0:T(8,128)} custom-call(s32[64]{0:T(128)} %order_ref.1, f32[64]{0:T(128)} %reshape.3.speed_ref, f32[2,8,64,2,8,128]{5,4,3,2,1,0:T(8,128)} %weights_ref.1, bf16[24,2,256,256]{3,2,1,0:T(8,128)(2,1)} %constant.4.clone.mats_ref, f32[2,8,128]{2,1,0:T(8,128)} %constant.5.clone.nodes_ref), custom_call_target="tpu_custom_call" | custom-call | tf_op jit(solution)/shard_map/pallas_call | solution.py:328
  221.7 7.7 %copy.7 = f32[2,16,32,2,8,128]{5,4,3,2,1,0:T(8,128)} copy(f32[2,16,32,2,8,128]{5,4,3,2,1,0:T(8,128)} %shard_map.55) | data formatting | bytes 16777216

commit v2 on v1

--- a/solution.py
+++ b/solution.py
@@ -15,6 +15,7 @@
 SUPERS = 4
 
 MESH = pl.DeviceIdType.MESH
+REGROUP = -1
 level_bits = (3, 2, 1, 0)
 
 
@@ -81,6 +82,10 @@
     return 1.0 - 2.0 * sine * sine, 2.0 * sine * cosine
 
 
+def late_chunks(chunks):
+    return chunks // 3
+
+
 def split_two(value):
     first = value.astype(jnp.bfloat16)
     return first, (value - first.astype(jnp.float32)).astype(jnp.bfloat16)
@@ -94,13 +99,18 @@
     sizes,
     order_ref,
     speed_ref,
+    weights_in_ref,
+    all_mats_ref,
+    nodes_ref,
+    out_ref,
     weights_ref,
     mats_ref,
-    nodes_ref,
-    out_ref,
     held,
     outgoing,
     arrived,
+    grouped,
+    weights_sem,
+    mats_sem,
     send_sem,
     recv_sem,
     far_send,
@@ -114,6 +124,7 @@
     chunks = slots * parts
     across_boxes = 8 * narrow
     boxes = narrow * codes * SUPERS
+    first_grouped = late_chunks(chunks)
     wide_place = lax.axis_index("wide")
     narrow_place = lax.axis_index("narrow")
 
@@ -124,11 +135,25 @@
         step = 1 << (level_bits[level] - local_bits)
         return wide_place + step * (1 - 2 * device_bit(level))
 
-    def matrix(level, target, child):
+    copies = [pltpu.make_async_copy(weights_in_ref, weights_ref, weights_sem)]
+    wanted = []
+    for level in range(partner_levels):
+        wanted.append((level, device_bit(level), device_bit(level)))
+        wanted.append((level, 1 - device_bit(level), device_bit(level)))
+    for level in range(partner_levels, 4):
+        wanted.extend((level, target, child) for target in range(2) for child in range(2))
+    for place, (level, target, child) in enumerate(wanted):
         if level < 2:
-            place = 4 * level + 2 * target + child
+            source = 4 * level + 2 * target + child
         else:
-            place = 8 * level - 8 + 4 * device_bit(level - 2) + 2 * target + child
+            source = 8 * level - 8 + 4 * device_bit(level - 2) + 2 * target + child
+        copies.append(
+            pltpu.make_async_copy(all_mats_ref.at[source], mats_ref.at[place], mats_sem.at[place])
+        )
+    for copy in copies:
+        copy.start()
+
+    def matrix(place):
         return mats_ref[place, 0], mats_ref[place, 1]
 
     def far(step):
@@ -142,6 +167,8 @@
     for step in range(1, narrow):
         pl.semaphore_signal(barrier, inc=1, device_id={"narrow": far(step)}, device_id_type=MESH)
     pl.semaphore_wait(barrier, partner_levels + narrow - 1)
+    for copy in copies:
+        copy.wait()
 
     def swap(level, k):
         return pltpu.make_async_remote_copy(
@@ -153,33 +180,31 @@
             device_id_type=MESH,
         )
 
-    def place_of(k):
-        return out_ref.at[
-            :, k // parts, pl.ds(narrow_place * supers + lax.rem(k, parts) * SUPERS, SUPERS)
-        ]
-
-    def hand_over(step, k):
+    def place_of(k, z):
+        return out_ref.at[:, k // parts, pl.ds(z * supers + lax.rem(k, parts) * SUPERS, SUPERS)]
+
+    def hand_over(step, k, late):
         return pltpu.make_async_remote_copy(
             src_ref=outgoing.at[k, far(step)],
-            dst_ref=place_of(k),
+            dst_ref=place_of(k, narrow_place) if late else grouped.at[k - first_grouped, narrow_place],
             send_sem=far_send.at[step - 1, k],
             recv_sem=far_recv.at[step - 1, k],
             device_id={"narrow": far(step)},
             device_id_type=MESH,
         )
 
-    def hand_own(k):
-        return pltpu.make_async_copy(outgoing.at[k, narrow_place], place_of(k), own_sem.at[k])
+    def write_out(k, z):
+        return pltpu.make_async_copy(outgoing.at[k, z], place_of(k, z), own_sem.at[z, k])
 
     def target_of(slot):
         box = order_ref[slot]
-        speed = speed_ref[box]
+        speed = speed_ref[box // TY, box % TY]
         center_across = ((box // TY).astype(jnp.float32) + 0.5) * np.float32(1.0 / TX)
         center_down = ((box % TY).astype(jnp.float32) + 0.5) * np.float32(1.0 / TY)
         return box, center_across, center_down, speed * np.float32(across_boxes / 4.0)
 
-    def radial(k, index, offset_across, offset_down):
-        place = narrow_place * supers + lax.rem(k, parts) * SUPERS + index
+    def radial(k, z, index, offset_across, offset_down):
+        place = z * supers + lax.rem(k, parts) * SUPERS + index
         corner_across = (4 * (place // SYH)).astype(jnp.float32)
         corner_down = (4 * (place % SYH)).astype(jnp.float32)
         unit_across = np.float32(1.0 / across_boxes)
@@ -225,13 +250,17 @@
             into[k, :, :, :, 1] = total[:, 128:].reshape(shape)
 
     def exchange(level, k, value):
-        bit = device_bit(level)
         split = along_first(value) if level % 2 == 0 else along_second(value)
-        store(outgoing, level, k, split, matrix(level, 1 - bit, bit))
+        store(outgoing, level, k, split, matrix(2 * level + 1))
         swap(level, k).start()
-        store(held, level, k, split, matrix(level, bit, bit))
-
-    def enter(k):
+        store(held, level, k, split, matrix(2 * level))
+
+    def regroup(k):
+        for step in range(1, narrow):
+            hand_over(step, k, False).start()
+        grouped[k - first_grouped, narrow_place] = outgoing[k, narrow_place]
+
+    def phased(k, into):
         base_super = lax.rem(k, parts) * SUPERS
         targets = [target_of(z * slots + k // parts) for z in range(narrow)]
         for code in range(codes):
@@ -243,71 +272,106 @@
             across = (offset_across - 2.0) * 0.25
             down = (offset_down - 2.0) * down_scale
             for index in range(SUPERS):
-                lengths = radial(k, index, offset_across, offset_down)
+                lengths = radial(k, narrow_place, index, offset_across, offset_down)
                 for z, (box, center_across, center_down, speed) in enumerate(targets):
                     cosine, sine = turned(
                         center_across * across + center_down * down + speed * lengths
                     )
                     real = weights_ref[code, base_super + index, box, 0]
                     imag = weights_ref[code, base_super + index, box, 1]
-                    held[k, z, code, index, 0] = real * cosine + imag * sine
-                    held[k, z, code, index, 1] = imag * cosine - real * sine
-        exchange(0, k, held[k])
-
-    def middle(level, k):
-        swap(level - 1, k).wait()
-        exchange(level, k, held[k] + arrived[level - 1, k])
-
-    def leave(k):
-        swap(partner_levels - 1, k).wait()
-        value = held[k] + arrived[partner_levels - 1, k]
+                    into[k, z, code, index, 0] = real * cosine + imag * sine
+                    into[k, z, code, index, 1] = imag * cosine - real * sine
+
+    def finished(k, value, late):
         results = []
         if partner_levels == 4:
             results.append((value[:, 0, :, 0], value[:, 0, :, 1]))
         else:
             splits = [along_second(value[:, child : child + 1]) for child in range(2)]
             for target in range(2):
-                total = second_product(splits[0], matrix(3, target, 0))
-                total = total + second_product(splits[1], matrix(3, target, 1))
+                total = second_product(splits[0], matrix(6 + 2 * target))
+                total = total + second_product(splits[1], matrix(7 + 2 * target))
                 shape = (narrow, SUPERS, 8, 128)
                 results.append((total[:, :128].reshape(shape), total[:, 128:].reshape(shape)))
-        targets = [target_of(z * slots + k // parts) for z in range(narrow)]
         across = nodes_across - 0.5
         down = (4.0 * nodes_down - 2.0) * down_scale
-        for index in range(SUPERS):
-            lengths = radial(k, index, 4.0 * nodes_across, 4.0 * nodes_down)
-            for z, (_, center_across, center_down, speed) in enumerate(targets):
-                cosine, sine = turned(
-                    center_across * across + center_down * down + speed * lengths
-                )
+        for z in range(narrow):
+            slot = (z if late else narrow_place) * slots + k // parts
+            _, center_across, center_down, speed = target_of(slot)
+            linear = center_across * across + center_down * down
+            for index in range(SUPERS):
+                source = narrow_place if late else z
+                lengths = radial(k, source, index, 4.0 * nodes_across, 4.0 * nodes_down)
+                cosine, sine = turned(linear + speed * lengths)
                 for code, (real, imag) in enumerate(results):
                     real, imag = real[z, index], imag[z, index]
                     outgoing[k, z, code, index, 0] = real * cosine - imag * sine
                     outgoing[k, z, code, index, 1] = real * sine + imag * cosine
+
+    def stage(steps, place, k):
+        late = REGROUP not in steps
+        if place == 0:
+            if steps[0] == REGROUP:
+                phased(k, outgoing)
+                regroup(k)
+            else:
+                phased(k, held)
+                exchange(steps[0], k, held[k])
+            return
+        before = steps[place - 1]
+        if before == REGROUP:
+            for step in range(1, narrow):
+                hand_over(step, k, False).wait()
+            value = grouped[k - first_grouped]
+        else:
+            swap(before, k).wait()
+            value = held[k] + arrived[before, k]
+        if place == len(steps):
+            finished(k, value, late)
+            if late:
+                for step in range(1, narrow):
+                    hand_over(step, k, True).start()
+                write_out(k, narrow_place).start()
+            else:
+                for z in range(narrow):
+                    write_out(k, z).start()
+        elif steps[place] == REGROUP:
+            outgoing[k] = value
+            regroup(k)
+        else:
+            exchange(steps[place], k, value)
+
+    rest = tuple(range(2, partner_levels))
+    orders = [((0, 1) + rest, 0, first_grouped)]
+    middle = first_grouped + (chunks - first_grouped) // 2
+    orders.append(((1, REGROUP, 0) + rest, first_grouped, middle))
+    orders.append(((REGROUP, 0, 1) + rest, middle, chunks))
+    depth = max(len(steps) for steps, _, _ in orders)
+    turns = max(last - first for _, first, last in orders)
+
+    def turn(now, carry):
+        for place in range(depth + 1):
+            for steps, first, last in orders:
+                if place <= len(steps):
+                    k = first + now - place
+                    pl.when((k >= first) & (k < last))(functools.partial(stage, steps, place, k))
+        return carry
+
+    lax.fori_loop(0, turns + depth, turn, 0)
+
+    def finish_late(k, carry):
         for step in range(1, narrow):
-            hand_over(step, k).start()
-        hand_own(k).start()
-
-    stages = [(0, enter)]
-    for level in range(1, partner_levels):
-        stages.append((2 * level, functools.partial(middle, level)))
-    stages.append((2 * partner_levels - 1, leave))
-
-    def turn(now, carry):
-        for lag, stage in stages:
-            k = now - lag
-            pl.when((k >= 0) & (k < chunks))(functools.partial(stage, k))
+            hand_over(step, k, True).wait()
+        write_out(k, narrow_place).wait()
         return carry
 
-    lax.fori_loop(0, chunks + stages[-1][0], turn, 0)
-
     def finish(k, carry):
-        for step in range(1, narrow):
-            hand_over(step, k).wait()
-        hand_own(k).wait()
+        for z in range(narrow):
+            write_out(k, z).wait()
         return carry
 
-    lax.fori_loop(0, chunks, finish, 0)
+    lax.fori_loop(first_grouped, chunks, finish, 0)
+    lax.fori_loop(0, first_grouped, finish_late, 0)
 
 
 def local(weights_in, medium_speed, target_order):
@@ -325,29 +389,36 @@
     sizes = (wide, narrow, codes, supers, slots)
     scalars = pl.BlockSpec(memory_space=pltpu.SMEM)
     vectors = pl.BlockSpec(memory_space=pltpu.VMEM)
+    anywhere = pl.BlockSpec(memory_space=pl.ANY)
+    matrices = 2 * partner_levels + 4 * (4 - partner_levels)
     return pl.pallas_call(
         functools.partial(kernel, sizes),
         out_shape=jax.ShapeDtypeStruct(
             (codes, slots, supers * narrow) + weights_in.shape[3:], jnp.float32
         ),
-        in_specs=[scalars, scalars, vectors, vectors, vectors],
-        out_specs=pl.BlockSpec(memory_space=pl.ANY),
+        in_specs=[scalars, scalars, anywhere, anywhere, vectors],
+        out_specs=anywhere,
         scratch_shapes=[
+            pltpu.VMEM(weights_in.shape, jnp.float32),
+            pltpu.VMEM((matrices, 2, 256, 256), jnp.bfloat16),
             pltpu.VMEM((chunks,) + chunk_shape, jnp.float32),
             pltpu.VMEM((chunks,) + chunk_shape, jnp.float32),
             pltpu.VMEM((partner_levels, chunks) + chunk_shape, jnp.float32),
+            pltpu.VMEM((chunks - late_chunks(chunks),) + chunk_shape, jnp.float32),
+            pltpu.SemaphoreType.DMA,
+            pltpu.SemaphoreType.DMA((matrices,)),
             pltpu.SemaphoreType.DMA((partner_levels, chunks)),
             pltpu.SemaphoreType.DMA((partner_levels, chunks)),
             pltpu.SemaphoreType.DMA((narrow - 1, chunks)),
             pltpu.SemaphoreType.DMA((narrow - 1, chunks)),
-            pltpu.SemaphoreType.DMA((chunks,)),
+            pltpu.SemaphoreType.DMA((narrow, chunks)),
         ],
         compiler_params=pltpu.CompilerParams(
             collective_id=0, has_side_effects=True, vmem_limit_bytes=62 * 2**20
         ),
     )(
         target_order,
-        medium_speed.reshape(-1),
+        medium_speed,
         weights_in,
         jnp.asarray(all_matrices(8 * narrow)),
         jnp.asarray(node_table),

time: 230 us -> 206 us (0.90)
  Pallas kernels: 220 us -> 198 us
    pallas_call x1, Pallas kernels: 220 us -> 198 us  [local(): pl.pallas_call(functools.partial(kernel, sizes), out_shape=jax.ShapeDtype...]
where the time goes in v2:
time: 206 us
  Pallas kernels  198 us (96%)
  local copies, waits for them, and re-layouts  7.65 us (4%)
    pallas_call x1, Pallas kernels, local(): pl.pallas_call(functools.partial(kernel, sizes), out_shape=jax.ShapeDtype...  198 us
    unnamed x1, local copies, waits for them, and re-layouts  7.65 us

profile of v2, /device:TPU:0, one launch (start us, length us, event | category | flops | bytes accessed | tf_op | source)
XLA Modules:
  0.0 205.5 jit_solution(4343700452791222102)
XLA Ops:
  0.0 197.8 %shard_map.55 = f32[2,16,32,2,8,128]{5,4,3,2,1,0:T(8,128)} custom-call(s32[64]{0:T(128)} %order_ref.1, f32[8,8]{1,0:T(8,128)} %speed_ref.1, f32[2,8,64,2,8,128]{5,4,3,2,1,0:T(8,128)} %weights_in_ref.1, bf16[24,2,256,256]{3,2,1,0:T(8,128)(2,1)} %constant.4.clone.all_mats_ref, f32[2,8,128]{2,1,0:T(8,128)} %constant.5.clone.nodes_ref), custom_call_target="tpu_custom_call" | custom-call | tf_op jit(solution)/shard_map/pallas_call | solution.py:394
  197.9 7.7 %copy.7 = f32[2,16,32,2,8,128]{5,4,3,2,1,0:T(8,128)} copy(f32[2,16,32,2,8,128]{5,4,3,2,1,0:T(8,128)} %shard_map.55) | data formatting | bytes 16777216

commit v3 on v2

--- a/solution.py
+++ b/solution.py
@@ -83,7 +83,7 @@
 
 
 def late_chunks(chunks):
-    return chunks // 3
+    return (chunks + 1) // 3
 
 
 def split_two(value):
@@ -135,7 +135,15 @@
         step = 1 << (level_bits[level] - local_bits)
         return wide_place + step * (1 - 2 * device_bit(level))
 
-    copies = [pltpu.make_async_copy(weights_in_ref, weights_ref, weights_sem)]
+    copies = []
+    for code in range(codes):
+        for part in range(parts):
+            piece = (code, pl.ds(part * SUPERS, SUPERS))
+            copies.append(
+                pltpu.make_async_copy(
+                    weights_in_ref.at[piece], weights_ref.at[piece], weights_sem.at[code, part]
+                )
+            )
     wanted = []
     for level in range(partner_levels):
         wanted.append((level, device_bit(level), device_bit(level)))
@@ -224,10 +232,11 @@
     def along_first(value):
         rows = value.reshape(boxes * 16, 128)
         pieces = [rows[256 * n : 256 * n + 256] for n in range(boxes // 16)]
-        return split_two(jnp.concatenate(pieces, axis=1))
+        first, rest = split_two(jnp.concatenate(pieces, axis=1))
+        return jnp.concatenate([first, rest, first], axis=0)
 
     def first_product(split, pair):
-        total = dot(pair[0], split[0]) + dot(pair[0], split[1]) + dot(pair[1], split[0])
+        total = dot(jnp.concatenate([pair[0], pair[0], pair[1]], axis=1), split)
         pieces = [total[:, 128 * n : 128 * n + 128] for n in range(boxes // 16)]
         return jnp.concatenate(pieces, axis=0).reshape(narrow, codes, SUPERS, 2, 8, 128)
 
@@ -235,10 +244,12 @@
         count = value.shape[0] * value.shape[1] * value.shape[2] * 8
         real = value[:, :, :, 0].reshape(count, 128)
         imag = value[:, :, :, 1].reshape(count, 128)
-        return split_two(jnp.concatenate([real, imag], axis=1))
-
-    def second_product(split, pair):
-        return dot(split[0], pair[0]) + dot(split[1], pair[0]) + dot(split[0], pair[1])
+        first, rest = split_two(jnp.concatenate([real, imag], axis=1))
+        return jnp.concatenate([first, rest, first], axis=1)
+
+    def second_product(split, *pairs):
+        terms = [term for pair in pairs for term in (pair[0], pair[0], pair[1])]
+        return dot(split, jnp.concatenate(terms, axis=0))
 
     def store(into, level, k, split, pair):
         if level % 2 == 0:
@@ -288,9 +299,9 @@
             results.append((value[:, 0, :, 0], value[:, 0, :, 1]))
         else:
             splits = [along_second(value[:, child : child + 1]) for child in range(2)]
+            split = jnp.concatenate(splits, axis=1)
             for target in range(2):
-                total = second_product(splits[0], matrix(6 + 2 * target))
-                total = total + second_product(splits[1], matrix(7 + 2 * target))
+                total = second_product(split, matrix(6 + 2 * target), matrix(7 + 2 * target))
                 shape = (narrow, SUPERS, 8, 128)
                 results.append((total[:, :128].reshape(shape), total[:, 128:].reshape(shape)))
         across = nodes_across - 0.5
@@ -341,11 +352,11 @@
         else:
             exchange(steps[place], k, value)
 
-    rest = tuple(range(2, partner_levels))
-    orders = [((0, 1) + rest, 0, first_grouped)]
-    middle = first_grouped + (chunks - first_grouped) // 2
-    orders.append(((1, REGROUP, 0) + rest, first_grouped, middle))
-    orders.append(((REGROUP, 0, 1) + rest, middle, chunks))
+    rest = tuple(range(3, partner_levels))
+    orders = [((0, 2, 1) + rest, 0, first_grouped)]
+    middle = first_grouped + chunks // 3
+    orders.append(((1, REGROUP, 0, 2) + rest, first_grouped, middle))
+    orders.append(((REGROUP, 0, 2, 1) + rest, middle, chunks))
     depth = max(len(steps) for steps, _, _ in orders)
     turns = max(last - first for _, first, last in orders)
 
@@ -405,7 +416,7 @@
             pltpu.VMEM((chunks,) + chunk_shape, jnp.float32),
             pltpu.VMEM((partner_levels, chunks) + chunk_shape, jnp.float32),
             pltpu.VMEM((chunks - late_chunks(chunks),) + chunk_shape, jnp.float32),
-            pltpu.SemaphoreType.DMA,
+            pltpu.SemaphoreType.DMA((codes, supers // SUPERS)),
             pltpu.SemaphoreType.DMA((matrices,)),
             pltpu.SemaphoreType.DMA((partner_levels, chunks)),
             pltpu.SemaphoreType.DMA((partner_levels, chunks)),

time: 206 us -> 217 us (1.053)
  Pallas kernels: 198 us -> 209 us
    pallas_call x1, Pallas kernels: 198 us -> 209 us  [local(): pl.pallas_call(functools.partial(kernel, sizes), out_shape=jax.ShapeDtype...]
where the time goes in v3:
time: 217 us; the launch traced here: 216 us
  Pallas kernels  209 us (96%)
  local copies, waits for them, and re-layouts  7.65 us (4%)
    pallas_call x1, Pallas kernels, local(): pl.pallas_call(functools.partial(kernel, sizes), out_shape=jax.ShapeDtype...  209 us
    unnamed x1, local copies, waits for them, and re-layouts  7.65 us

profile of v3, /device:TPU:0, one launch (start us, length us, event | category | flops | bytes accessed | tf_op | source)
XLA Modules:
  0.0 216.5 jit_solution(18003039092505729097)
XLA Ops:
  0.0 208.8 %shard_map.55 = f32[2,16,32,2,8,128]{5,4,3,2,1,0:T(8,128)} custom-call(s32[64]{0:T(128)} %order_ref.1, f32[8,8]{1,0:T(8,128)} %speed_ref.1, f32[2,8,64,2,8,128]{5,4,3,2,1,0:T(8,128)} %weights_in_ref.1, bf16[24,2,256,256]{3,2,1,0:T(8,128)(2,1)} %constant.4.clone.all_mats_ref, f32[2,8,128]{2,1,0:T(8,128)} %constant.5.clone.nodes_ref), custom_call_target="tpu_custom_call" | custom-call | tf_op jit(solution)/shard_map/pallas_call | solution.py:405
  208.8 7.7 %copy.7 = f32[2,16,32,2,8,128]{5,4,3,2,1,0:T(8,128)} copy(f32[2,16,32,2,8,128]{5,4,3,2,1,0:T(8,128)} %shard_map.55) | data formatting | bytes 16777216

commit v4 on v3

--- a/solution.py
+++ b/solution.py
@@ -232,11 +232,10 @@
     def along_first(value):
         rows = value.reshape(boxes * 16, 128)
         pieces = [rows[256 * n : 256 * n + 256] for n in range(boxes // 16)]
-        first, rest = split_two(jnp.concatenate(pieces, axis=1))
-        return jnp.concatenate([first, rest, first], axis=0)
+        return split_two(jnp.concatenate(pieces, axis=1))
 
     def first_product(split, pair):
-        total = dot(jnp.concatenate([pair[0], pair[0], pair[1]], axis=1), split)
+        total = dot(pair[0], split[0]) + dot(pair[0], split[1]) + dot(pair[1], split[0])
         pieces = [total[:, 128 * n : 128 * n + 128] for n in range(boxes // 16)]
         return jnp.concatenate(pieces, axis=0).reshape(narrow, codes, SUPERS, 2, 8, 128)
 
@@ -244,12 +243,10 @@
         count = value.shape[0] * value.shape[1] * value.shape[2] * 8
         real = value[:, :, :, 0].reshape(count, 128)
         imag = value[:, :, :, 1].reshape(count, 128)
-        first, rest = split_two(jnp.concatenate([real, imag], axis=1))
-        return jnp.concatenate([first, rest, first], axis=1)
-
-    def second_product(split, *pairs):
-        terms = [term for pair in pairs for term in (pair[0], pair[0], pair[1])]
-        return dot(split, jnp.concatenate(terms, axis=0))
+        return split_two(jnp.concatenate([real, imag], axis=1))
+
+    def second_product(split, pair):
+        return dot(split[0], pair[0]) + dot(split[1], pair[0]) + dot(split[0], pair[1])
 
     def store(into, level, k, split, pair):
         if level % 2 == 0:
@@ -299,9 +296,9 @@
             results.append((value[:, 0, :, 0], value[:, 0, :, 1]))
         else:
             splits = [along_second(value[:, child : child + 1]) for child in range(2)]
-            split = jnp.concatenate(splits, axis=1)
             for target in range(2):
-                total = second_product(split, matrix(6 + 2 * target), matrix(7 + 2 * target))
+                total = second_product(splits[0], matrix(6 + 2 * target))
+                total = total + second_product(splits[1], matrix(7 + 2 * target))
                 shape = (narrow, SUPERS, 8, 128)
                 results.append((total[:, :128].reshape(shape), total[:, 128:].reshape(shape)))
         across = nodes_across - 0.5

time: 217 us -> 217 us (level)
  no operation moved by 1% of the time
where the time goes in v4:
time: 217 us; the launch traced here: 216 us
  Pallas kernels  209 us (96%)
  local copies, waits for them, and re-layouts  7.65 us (4%)
    pallas_call x1, Pallas kernels, local(): pl.pallas_call(functools.partial(kernel, sizes), out_shape=jax.ShapeDtype...  209 us
    unnamed x1, local copies, waits for them, and re-layouts  7.65 us

profile of v4, /device:TPU:0, one launch (start us, length us, event | category | flops | bytes accessed | tf_op | source)
XLA Modules:
  0.0 216.5 jit_solution(6387933955559206942)
XLA Ops:
  0.0 208.8 %shard_map.55 = f32[2,16,32,2,8,128]{5,4,3,2,1,0:T(8,128)} custom-call(s32[64]{0:T(128)} %order_ref.1, f32[8,8]{1,0:T(8,128)} %speed_ref.1, f32[2,8,64,2,8,128]{5,4,3,2,1,0:T(8,128)} %weights_in_ref.1, bf16[24,2,256,256]{3,2,1,0:T(8,128)(2,1)} %constant.4.clone.all_mats_ref, f32[2,8,128]{2,1,0:T(8,128)} %constant.5.clone.nodes_ref), custom_call_target="tpu_custom_call" | custom-call | tf_op jit(solution)/shard_map/pallas_call | solution.py:402
  208.8 7.7 %copy.7 = f32[2,16,32,2,8,128]{5,4,3,2,1,0:T(8,128)} copy(f32[2,16,32,2,8,128]{5,4,3,2,1,0:T(8,128)} %shard_map.55) | data formatting | bytes 16777216

commit v5 on v4

--- a/solution.py
+++ b/solution.py
@@ -349,23 +349,28 @@
         else:
             exchange(steps[place], k, value)
 
-    rest = tuple(range(3, partner_levels))
-    orders = [((0, 2, 1) + rest, 0, first_grouped)]
+    rest = tuple(range(2, partner_levels))
+    orders = [((0, 1) + rest, 0, first_grouped)]
     middle = first_grouped + chunks // 3
-    orders.append(((1, REGROUP, 0, 2) + rest, first_grouped, middle))
-    orders.append(((REGROUP, 0, 2, 1) + rest, middle, chunks))
-    depth = max(len(steps) for steps, _, _ in orders)
+    orders.append(((1, REGROUP, 0) + rest, first_grouped, middle))
+    orders.append(((REGROUP, 0, 1) + rest, middle, chunks))
     turns = max(last - first for _, first, last in orders)
 
+    plan = []
+    for number, (steps, _, _) in enumerate(orders):
+        for place in range(len(steps) + 1):
+            lag = sum(step != partner_levels - 1 for step in steps[:place])
+            plan.append((lag, place, number))
+    plan.sort()
+
     def turn(now, carry):
-        for place in range(depth + 1):
-            for steps, first, last in orders:
-                if place <= len(steps):
-                    k = first + now - place
-                    pl.when((k >= first) & (k < last))(functools.partial(stage, steps, place, k))
+        for lag, place, number in plan:
+            steps, first, last = orders[number]
+            k = first + now - lag
+            pl.when((k >= first) & (k < last))(functools.partial(stage, steps, place, k))
         return carry
 
-    lax.fori_loop(0, turns + depth, turn, 0)
+    lax.fori_loop(0, turns + plan[-1][0], turn, 0)
 
     def finish_late(k, carry):
         for step in range(1, narrow):

time: 217 us -> 207 us (0.954)
  Pallas kernels: 209 us -> 199 us
    pallas_call x1, Pallas kernels: 209 us -> 199 us  [local(): pl.pallas_call(functools.partial(kernel, sizes), out_shape=jax.ShapeDtype...]
where the time goes in v5:
time: 207 us
  Pallas kernels  199 us (96%)
  local copies, waits for them, and re-layouts  7.65 us (4%)
    pallas_call x1, Pallas kernels, local(): pl.pallas_call(functools.partial(kernel, sizes), out_shape=jax.ShapeDtype...  199 us
    unnamed x1, local copies, waits for them, and re-layouts  7.65 us

profile of v5, /device:TPU:0, one launch (start us, length us, event | category | flops | bytes accessed | tf_op | source)
XLA Modules:
  0.0 207.1 jit_solution(15604024323263188920)
XLA Ops:
  0.0 199.4 %shard_map.55 = f32[2,16,32,2,8,128]{5,4,3,2,1,0:T(8,128)} custom-call(s32[64]{0:T(128)} %order_ref.1, f32[8,8]{1,0:T(8,128)} %speed_ref.1, f32[2,8,64,2,8,128]{5,4,3,2,1,0:T(8,128)} %weights_in_ref.1, bf16[24,2,256,256]{3,2,1,0:T(8,128)(2,1)} %constant.4.clone.all_mats_ref, f32[2,8,128]{2,1,0:T(8,128)} %constant.5.clone.nodes_ref), custom_call_target="tpu_custom_call" | custom-call | tf_op jit(solution)/shard_map/pallas_call | solution.py:407
  199.4 7.7 %copy.7 = f32[2,16,32,2,8,128]{5,4,3,2,1,0:T(8,128)} copy(f32[2,16,32,2,8,128]{5,4,3,2,1,0:T(8,128)} %shard_map.55) | data formatting | bytes 16777216
